TPU v7x, 256 devices: a whole 4x4x8 slice. The times are simulated.
256 devices in a mesh: seq: 64 (over y, z, core), tp: 4 (over x).
Axes of the slice: x: 4, y: 4, z: 8, core: 2. Of those that a mesh axis runs over, the one named last changes fastest.
Arguments:
- queries: bfloat16 [8192, 4096], P('seq', 'tp'), may hold values from -10 to 10
- key_vectors: bfloat16 [8192, 512], P('seq', 'tp'), may hold values from -8.5 to 8.5
- value_vectors: bfloat16 [8192, 512], P('seq', 'tp'), may hold values from -6 to 6
- vertical: int32 [32, 16], P('tp'), may hold values from 0 to 63
- vertical_count: int32 [32], P('tp'), may hold values from 1 to 16, as said below
- slash_offsets: int32 [32, 8], P('tp'), may hold values from 1 to 63
- out_weight: bfloat16 [4096, 5120], P('tp'), may hold values from -0.09375 to 0.09375
Outputs:
- output: bfloat16 [8192, 5120], P(('seq', 'tp'))
Inputs may be any that keep to these rules, and one draw needn't show every extreme that they name: `vertical_count`: a power of two for each head; 16 for some head in every draw.
All inputs are finite; a program needn't handle non-finite values.
Results may differ from a plain program's by a relative error of at most 0.019.
Values may be sent and summed in bfloat16 or wider, within the bound.
A program may use at most 128 MiB of HBM per device.

v0:
```python
import jax
import jax.numpy as jnp
from jax import lax
from jax.sharding import PartitionSpec as P

HEAD = 128
BLOCK = 128


def candidates(query_block, vert_row, allowed_count, slash_row):
    query_col = query_block[:, None]
    shifted = query_col - slash_row[None, :]
    upright = jnp.broadcast_to(vert_row[None, :], (query_block.shape[0], vert_row.shape[0]))
    listed = jnp.concatenate([query_col, shifted, upright], axis=1)
    slot_ids = jnp.arange(vert_row.shape[0], dtype=jnp.int32)
    usable = jnp.concatenate(
        [
            query_col >= 0,
            shifted >= 0,
            (upright <= query_col) & (slot_ids < allowed_count)[None, :],
        ],
        axis=1,
    )
    order_ids = jnp.arange(listed.shape[1], dtype=jnp.int32)
    before = order_ids[:, None] > order_ids[None, :]
    same = listed[:, :, None] == listed[:, None, :]
    repeated = jnp.any(same & before[None, :, :] & usable[:, None, :], axis=2)
    return (listed, usable & jnp.logical_not(repeated))


def pick_group(unit_total, sub_rows):
    target = max(1, 512 // sub_rows)
    chosen_size = min(unit_total, target)
    while unit_total % chosen_size:
        chosen_size = chosen_size - 1
    return chosen_size


def attend_groups(
    query_units,
    unit_starts,
    unit_heads,
    key_blocks,
    value_blocks,
    vertical,
    vertical_count,
    slash_offsets,
):
    sub_rows = query_units.shape[2]
    group_size = vertical.shape[0] // key_blocks.shape[0]
    block_total = key_blocks.shape[1]
    fixed_width = 1 + slash_offsets.shape[1]
    score_scale = HEAD ** (-0.5)

    def one_group(packed):
        query_tile, starts, head_id = packed
        kv_head = head_id // group_size
        query_block = starts // BLOCK
        query_pos = starts[:, None] + jnp.arange(sub_rows, dtype=jnp.int32)[None, :]
        vert_row = vertical[head_id]
        allowed_count = vertical_count[head_id]
        listed, kept_blocks = candidates(
            query_block, vert_row, allowed_count, slash_offsets[head_id]
        )
        fixed_ids = jnp.clip(listed[:, :fixed_width], 0, block_total - 1)
        fixed_keys = key_blocks[kv_head, fixed_ids]
        fixed_values = value_blocks[kv_head, fixed_ids]
        fixed_scores = (
            jnp.einsum("usd,uckd->usck", query_tile, fixed_keys, preferred_element_type=jnp.float32)
            * score_scale
        )
        key_pos = (
            fixed_ids[:, None, :, None] * BLOCK
            + jnp.arange(BLOCK, dtype=jnp.int32)[None, None, None, :]
        )
        fixed_mask = kept_blocks[:, None, :fixed_width, None] & (
            key_pos <= query_pos[:, :, None, None]
        )
        fixed_scores = jnp.where(fixed_mask, fixed_scores, -jnp.inf)

        def vertical_scores(slot_id):
            key_tile = key_blocks[kv_head, vert_row[slot_id]]
            scores = (
                jnp.einsum("usd,kd->usk", query_tile, key_tile, preferred_element_type=jnp.float32)
                * score_scale
            )
            column = lax.dynamic_index_in_dim(kept_blocks, fixed_width + slot_id, 1, keepdims=False)
            return jnp.where(column[:, None, None], scores, -jnp.inf)

        first_max = jnp.max(fixed_scores, axis=(2, 3))
        first_sum = jnp.sum(jnp.exp(fixed_scores - first_max[:, :, None, None]), axis=(2, 3))

        def stats_step(slot_id, state_pair):
            row_max, row_sum = state_pair
            scores = vertical_scores(slot_id)
            new_max = jnp.maximum(row_max, jnp.max(scores, axis=2))
            row_sum = row_sum * jnp.exp(row_max - new_max) + jnp.sum(
                jnp.exp(scores - new_max[:, :, None]), axis=2
            )
            return (new_max, row_sum)

        row_max, row_sum = lax.fori_loop(0, allowed_count, stats_step, (first_max, first_sum))
        fixed_weights = (
            jnp.exp(fixed_scores - row_max[:, :, None, None]) / row_sum[:, :, None, None]
        ).astype(jnp.bfloat16)
        summed = jnp.einsum(
            "usck,uckd->usd", fixed_weights, fixed_values, preferred_element_type=jnp.float32
        )

        def value_step(slot_id, running):
            scores = vertical_scores(slot_id)
            weights = (jnp.exp(scores - row_max[:, :, None]) / row_sum[:, :, None]).astype(
                jnp.bfloat16
            )
            value_tile = value_blocks[kv_head, vert_row[slot_id]]
            return running + jnp.einsum(
                "usk,kd->usd", weights, value_tile, preferred_element_type=jnp.float32
            )

        summed = lax.fori_loop(0, allowed_count, value_step, summed)
        return summed.astype(jnp.bfloat16)

    return lax.map(one_group, (query_units, unit_starts, unit_heads))


def owner_path(query_heads, key_blocks, value_blocks, vertical, vertical_count, slash_offsets):
    seq_count = lax.axis_size("seq")
    my_index = lax.axis_index("seq")
    local_rows = query_heads.shape[0]
    heads_here = query_heads.shape[1]
    row_groups = seq_count // heads_here
    piece_rows = local_rows // row_groups
    outgoing = query_heads
    outgoing = (
        outgoing.reshape(row_groups, piece_rows, heads_here, HEAD)
        .transpose(2, 0, 1, 3)
        .reshape(seq_count, piece_rows, HEAD)
    )
    incoming = lax.all_to_all(outgoing, "seq", split_axis=0, concat_axis=0, tiled=True)
    my_head = my_index // row_groups
    my_group = my_index % row_groups
    sub_rows = min(piece_rows, BLOCK)
    per_piece = piece_rows // sub_rows
    half_units = seq_count // 2 * per_piece
    group_units = pick_group(half_units, sub_rows)
    source_ids = jnp.arange(seq_count, dtype=jnp.int32)
    starts = (
        source_ids[:, None] * local_rows
        + my_group * piece_rows
        + jnp.arange(per_piece, dtype=jnp.int32)[None, :] * sub_rows
    )
    query_units = (
        incoming.reshape(seq_count // 2, 2, per_piece, sub_rows, HEAD)
        .transpose(1, 0, 2, 3, 4)
        .reshape(-1, group_units, sub_rows, HEAD)
    )
    unit_starts = (
        starts.reshape(seq_count // 2, 2, per_piece).transpose(1, 0, 2).reshape(-1, group_units)
    )
    unit_heads = jnp.repeat(jnp.stack([my_head, my_head]), half_units // group_units)
    result = attend_groups(
        query_units,
        unit_starts,
        unit_heads,
        key_blocks,
        value_blocks,
        vertical,
        vertical_count,
        slash_offsets,
    )
    result = (
        result.reshape(2, seq_count // 2, per_piece, sub_rows, HEAD)
        .transpose(1, 0, 2, 3, 4)
        .reshape(seq_count, piece_rows, HEAD)
    )
    returned = lax.all_to_all(result, "seq", split_axis=0, concat_axis=0, tiled=True)
    returned = (
        returned.reshape(heads_here, row_groups, piece_rows, HEAD)
        .transpose(1, 2, 0, 3)
        .reshape(local_rows, heads_here, HEAD)
    )
    return returned


def body(queries, key_vectors, value_vectors, vertical, vertical_count, slash_offsets, out_weight):
    seq_count = lax.axis_size("seq")
    local_rows = queries.shape[0]
    heads_here = vertical.shape[0]
    kv_here = key_vectors.shape[1] // HEAD
    key_all, value_all = (
        lax.all_gather(key_vectors, "seq", axis=0, tiled=True),
        lax.all_gather(value_vectors, "seq", axis=0, tiled=True),
    )
    block_total = local_rows * seq_count // BLOCK
    key_blocks = key_all.reshape(block_total, BLOCK, kv_here, HEAD).transpose(2, 0, 1, 3)
    value_blocks = value_all.reshape(block_total, BLOCK, kv_here, HEAD).transpose(2, 0, 1, 3)
    query_heads = queries.reshape(local_rows, heads_here, HEAD)
    attended = owner_path(
        query_heads, key_blocks, value_blocks, vertical, vertical_count, slash_offsets
    )
    attended = attended.reshape(local_rows, heads_here * HEAD)
    return lax.psum_scatter(
        jnp.dot(attended, out_weight, preferred_element_type=jnp.float32).astype(jnp.bfloat16),
        "tp",
        scatter_dimension=0,
        tiled=True,
    )


def solution(mesh):
    in_specs = (
        P("seq", "tp"),
        P("seq", "tp"),
        P("seq", "tp"),
        P("tp", None),
        P("tp"),
        P("tp", None),
        P("tp", None),
    )
    out_specs = P(("seq", "tp"), None)
    return jax.shard_map(body, mesh=mesh, in_specs=in_specs, out_specs=out_specs, check_vma=False)
```

profile of v0, /device:TPU:24, one launch (start us, length us, event | category | flops | bytes accessed | tf_op | source)
XLA Modules:
  0.0 619.8 jit_solution(1403151289901075623)
XLA Ops:
  6.5 0.7 all-gather.3.cloned.1.call-update
  7.3 0.7 all-gather.5.cloned.1.call-update
  8.0 1.0 copy.93
  9.0 0.7 copy.84
  9.8 12.1 %all-to-all-start = ((bf16[64,16,128]{2,1,0:T(8,128)(2,1)}), bf16[64,16,128]{2,1,0:T(8,128)(2,1)S(1)}, u32[]{:S(2)}, u32[]{:S(2)}) async-start(bf16[64,16,128]{2,1,0:T(8,128)(2,1)} %bitcast.33), calls=%async_computation | async-start | bytes 524288 | tf_op jit(solution)/shard_map/all_to_all | solution.py:139
  22.1 11.6 %all-to-all-done = bf16[64,16,128]{2,1,0:T(8,128)(2,1)S(1)} async-done(((bf16[64,16,128]{2,1,0:T(8,128)(2,1)}), bf16[64,16,128]{2,1,0:T(8,128)(2,1)S(1)}, u32[]{:S(2)}, u32[]{:S(2)}) %all-to-all-start) | async-done | bytes 262176 | tf_op jit(solution)/shard_map/all_to_all | solution.py:139
  33.6 55.7 %all-gather.3.cloned.1.call-done = bf16[8192,128]{1,0:T(8,128)(2,1)} async-done(((bf16[128,128]{1,0:T(8,128)(2,1)}), bf16[8192,128]{1,0:T(8,128)(2,1)}) %all-gather.3.cloned.1.call-update) | async-done | bytes 2097168 | tf_op jit(solution)/shard_map/all_gather | solution.py:191
  89.3 77.8 %all-gather.5.cloned.1.call-done = bf16[8192,128]{1,0:T(8,128)(2,1)} async-done(((bf16[128,128]{1,0:T(8,128)(2,1)}), bf16[8192,128]{1,0:T(8,128)(2,1)}) %all-gather.5.cloned.1.call-update) | async-done | bytes 2097168 | tf_op jit(solution)/shard_map/all_gather | solution.py:192
  167.1 133.0 %while.59 = (s32[]{:T(128)}, bf16[2,32,16,128]{3,2,0,1:T(8,128)(2,1)S(1)}, s32[2,32]{1,0:T(2,128)S(1)}, s32[2]{0:T(128)S(1)}, s32[8,8]{1,0:T(8,128)}, /*index=5*...) while((s32[]{:T(128)}, ...), condition=%wide.region_10.11_spmd, body=%wide.region_0.10_spmd.sunk | while | flops 359135808 | bytes 84820456 | solution.py:123
  167.1 0.6 dynamic_slice.153
  171.4 0.7 fusion.65
  172.4 17.7 %gather_fusion.1 = bf16[288,128,128]{2,1,0:T(8,128)(2,1)} fusion(bf16[1,64,128,128]{3,2,1,0:T(8,128)(2,1)} %get-tuple-element.1096, s32[288]{0:T(512)S(1)} %reshape.430), kind=kCustom, calls=%fused_computation.clone.1 | custom fusion | bytes 18876672 | tf_op jit(solution)/shard_map/while/body/eval_jaxpr/gather | solution.py:66
  190.2 0.7 fusion.68
  190.9 0.6 dynamic_slice.154
  191.5 0.6 iota_compare_fusion.4
  192.6 0.7 and_reduce_fusion.2
  193.7 5.5 fusion.69
  199.1 1.4 copy-done.1
  200.5 0.5 exponential_reduce_fusion.4
  201.2 5.1 while.60
  201.9 0.6 dynamic_slice.157
  204.4 1.1 fusion.72
  206.5 16.1 %gather_fusion = bf16[288,128,128]{2,1,0:T(8,128)(2,1)} fusion(bf16[1,64,128,128]{3,2,1,0:T(8,128)(2,1)S(1)} %copy-done, s32[288]{0:T(512)S(1)} %reshape.430), kind=kCustom, calls=%fused_computation.1.clone.1 | custom fusion | bytes 18876672 | tf_op jit(solution)/shard_map/while/body/eval_jaxpr/gather | solution.py:67
  222.7 5.9 fusion.70
  228.6 4.9 while.61
  229.3 0.6 dynamic_slice.161
  231.8 1.1 convolution_add_fusion.2
  233.6 0.6 dynamic_slice.153
  237.9 0.7 fusion.65
  238.9 17.8 %gather_fusion.1 = bf16[288,128,128]{2,1,0:T(8,128)(2,1)} fusion(bf16[1,64,128,128]{3,2,1,0:T(8,128)(2,1)} %get-tuple-element.1096, s32[288]{0:T(512)S(1)} %reshape.430), kind=kCustom, calls=%fused_computation.clone.1 | custom fusion | bytes 18876672 | tf_op jit(solution)/shard_map/while/body/eval_jaxpr/gather | solution.py:66
  256.7 0.7 fusion.68
  257.4 0.6 dynamic_slice.154
  258.0 0.6 iota_compare_fusion.4
  259.1 0.7 and_reduce_fusion.2
  260.2 5.5 fusion.69
  265.7 1.4 copy-done.1
  267.1 0.5 exponential_reduce_fusion.4
  267.8 5.1 while.60
  268.4 0.6 dynamic_slice.157
  270.9 1.1 fusion.72
  273.1 16.1 %gather_fusion = bf16[288,128,128]{2,1,0:T(8,128)(2,1)} fusion(bf16[1,64,128,128]{3,2,1,0:T(8,128)(2,1)S(1)} %copy-done, s32[288]{0:T(512)S(1)} %reshape.430), kind=kCustom, calls=%fused_computation.1.clone.1 | custom fusion | bytes 18876672 | tf_op jit(solution)/shard_map/while/body/eval_jaxpr/gather | solution.py:67
  289.2 5.9 fusion.70
  295.2 4.9 while.61
  295.8 0.6 dynamic_slice.161
  298.3 1.1 convolution_add_fusion.2
  300.1 281.9 %all_to_all.10 = bf16[64,16,128]{2,1,0:T(8,128)(2,1)S(1)} all-to-all(bf16[64,16,128]{2,1,0:T(8,128)(2,1)S(1)} %bitcast.168), channel_id=1, replica_groups=mesh['seq'=64,'tp'=4] {'seq'}, dimensions={0} | all-to-all | bytes 524288 | tf_op jit(solution)/shard_map/all_to_all | solution.py:176
  582.2 6.6 %convolution_convert_fusion = bf16[128,5120]{1,0:T(8,128)(2,1)} fusion(bf16[1024,5120]{1,0:T(8,128)(2,1)} %param.19, bf16[16,8,8,128]{3,2,1,0:T(8,128)(2,1)S(1)} %bitcast.164), kind=kOutput, calls=%fused_computation.79 | convolution fusion | flops 1342832640 | bytes 12058624 | tf_op jit(solution)/shard_map/dot_general | solution.py:203
  588.9 24.5 %reduce-scatter.2.cloned.1.call-done = bf16[32,5120]{1,0:T(8,128)(2,1)} async-done(((bf16[128,5120]{1,0:T(8,128)(2,1)}), bf16[32,5120]{1,0:T(8,128)(2,1)}) %reduce-scatter.2.cloned.1.call-update) | async-done | bytes 327696 | tf_op jit(solution)/shard_map/reduce_scatter | solution.py:202
  (87 shorter events, 4.1 us)
Async XLA Ops:
  6.5 82.8 %all-gather.3.cloned.1.call-start = ((), (), s32[]{:S(2)}) async-start(), calls=%async_computation.3 | async-start | bytes 2129920 | tf_op jit(solution)/shard_map/all_gather | solution.py:191
  7.3 159.8 %all-gather.5.cloned.1.call-start = ((), (), s32[]{:S(2)}) async-start(), calls=%async_computation.4 | async-start | bytes 2129920 | tf_op jit(solution)/shard_map/all_gather | solution.py:192
  9.8 23.8 %all-to-all-start = ((bf16[64,16,128]{2,1,0:T(8,128)(2,1)}), bf16[64,16,128]{2,1,0:T(8,128)(2,1)S(1)}, u32[]{:S(2)}, u32[]{:S(2)}) async-start(bf16[64,16,128]{2,1,0:T(8,128)(2,1)} %bitcast.33), calls=%async_computation | async-start | bytes 524288 | tf_op jit(solution)/shard_map/all_to_all | solution.py:139
  21.9 591.4 %reduce-scatter.2.cloned.1.call-start = ((), (), s32[]{:S(2)}) async-start(), calls=%async_computation.5 | async-start | bytes 1638400 | tf_op jit(solution)/shard_map/reduce_scatter | solution.py:202
  172.4 18.4 %copy-start.2 = (s32[8]{0:T(128)S(1)}, s32[8]{0:T(128)}, u32[]{:S(2)}) copy-start(s32[8]{0:T(128)} %get-tuple-element.1094) | copy-start | bytes 100 | tf_op jit(solution)/shard_map/while
  199.1 1.4 copy-start.1
  200.5 6.0 copy-start
  238.9 18.5 %copy-start.2 = (s32[8]{0:T(128)S(1)}, s32[8]{0:T(128)}, u32[]{:S(2)}) copy-start(s32[8]{0:T(128)} %get-tuple-element.1094) | copy-start | bytes 100 | tf_op jit(solution)/shard_map/while
  265.7 1.4 copy-start.1
  267.1 6.0 copy-start
Sparse Core Ops, SparseCore 0:
  10.1 79.1 all-gather.2
  92.1 74.9 all-gather.4
  589.0 24.2 reduce-scatter.1
where the time goes:
time: 627 us; the launch traced here: 620 us
  blocking collectives  282 us (45%)
  waiting for transfers between devices  171 us (27%)
  local copies, waits for them, and re-layouts  82.2 us (13%)
  matrix products  33.8 us (5%)
  loops' own time  20.4 us (3%)
  between operations  13.2 us (2%)
  starting transfers between devices  12.2 us (2%)
    all_to_all x1, blocking collectives, owner_path(): lax.all_to_all(result, 'seq', split_axis=0, concat_axis=0, tiled=True)  282 us
    all_gather x1, waiting for transfers between devices, body(): lax.all_gather(value_vectors, 'seq', axis=0, tiled=True)  77.8 us
    all_gather x1, waiting for transfers between devices, body(): lax.all_gather(key_vectors, 'seq', axis=0, tiled=True)  55.7 us
    gather x2, local copies, waits for them, and re-layouts, one_group(): fixed_keys = key_blocks[kv_head, fixed_ids]  35.5 us
    gather x2, local copies, waits for them, and re-layouts, one_group(): fixed_values = value_blocks[kv_head, fixed_ids]  32.3 us
    reduce_scatter x1, waiting for transfers between devices, body(): lax.psum_scatter(jnp.dot(attended, out_weight, preferred_element_type=jnp...  24.5 us
  transfers between devices with their start and end apart: 4, of which 4 were waited for; matrix products, arithmetic and copies ran while one was open for 0% of the time, Pallas kernels for 0%

commit v1 on v0

v1 whole, which is shorter than its diff:
```python
import functools
import math

import jax
import jax.numpy as jnp
from jax import lax
from jax.experimental import pallas as pl
from jax.experimental.pallas import tpu as pltpu
from jax.sharding import PartitionSpec as P

HEAD = 128
BLOCK = 128
HEADS = 8
NY, NZ = 4, 8
NB = 64
HALF = NB // 2
NSLASH, NVERT = 8, 16
SLOTS = 1 + NSLASH + NVERT
D = 5120
PIECE = 512
SIDE = D // PIECE // 2
PIECES = 2 * SIDE
ROWS = 32
FEATURES = HEADS * HEAD
EXP2_SCALE = HEAD**-0.5 * math.log2(math.e)
MESH = pl.DeviceIdType.MESH
NEG = float("-inf")


def key_slot(core, y, z):
    return core * HALF + z * NY + y


def value_slot(core, y, z):
    return NB + core * HALF + y * NZ + z


def choose_blocks(head, me, vert_ref, count_ref, slash_ref, key_at, value_at, bias_at):
    low = jnp.where(me < 32, jnp.left_shift(jnp.int32(1), me % 32), 0)
    high = jnp.where(me < 32, 0, jnp.left_shift(jnp.int32(1), me % 32))
    count = count_ref[head]
    for c in range(1, SLOTS):
        if c <= NSLASH:
            block = me - slash_ref[head, c - 1]
            usable = block >= 0
        else:
            block = vert_ref[head, c - 1 - NSLASH]
            usable = (block <= me) & (c - 1 - NSLASH < count)
        block = jnp.clip(block, 0, NB - 1)
        bit = jnp.left_shift(jnp.int32(1), block % 32)
        in_low = block < 32
        seen = (jnp.where(in_low, low, high) & bit) != 0
        kept = usable & jnp.logical_not(seen)
        add = jnp.where(kept, bit, 0)
        low = low | jnp.where(in_low, add, 0)
        high = high | jnp.where(in_low, 0, add)
        core, z, y = block % 2, (block // 2) % NZ, block // (2 * NZ)
        key_at[head, c] = key_slot(core, y, z)
        value_at[head, c] = value_slot(core, y, z)
        bias_at[head, c] = jnp.where(kept, jnp.float32(0), jnp.float32(NEG))


def attend_head(head, q_vm, kv, key_at, value_at, bias_at, own_key, own_value, scores, att):
    query = q_vm[head]
    rows = lax.broadcasted_iota(jnp.int32, (BLOCK, BLOCK), 0)
    cols = lax.broadcasted_iota(jnp.int32, (BLOCK, BLOCK), 1)
    top = None
    for c in range(0, SLOTS, 2):
        slots = [c] if c + 1 == SLOTS else [c, c + 1]
        keys = [kv[own_key if s == 0 else key_at[head, s]] for s in slots]
        keys = keys[0] if len(keys) == 1 else jnp.concatenate(keys, axis=0)
        both = lax.dot_general(
            query, keys, (((1,), (1,)), ((), ())), preferred_element_type=jnp.float32
        )
        for n, s in enumerate(slots):
            part = both[:, n * BLOCK : (n + 1) * BLOCK]
            if s == 0:
                part = jnp.where(cols <= rows, part, NEG)
            else:
                part = part + bias_at[head, s]
            scores[:, s * BLOCK : (s + 1) * BLOCK] = part
            top = part if top is None else jnp.maximum(top, part)
    top = jnp.max(top, axis=1, keepdims=True)
    total, out = None, None
    for c in range(0, SLOTS, 2):
        slots = [c] if c + 1 == SLOTS else [c, c + 1]
        values = [kv[own_value if s == 0 else value_at[head, s]] for s in slots]
        values = values[0] if len(values) == 1 else jnp.concatenate(values, axis=0)
        wide = len(slots) * BLOCK
        weights = jnp.exp2((scores[:, c * BLOCK : c * BLOCK + wide] - top) * EXP2_SCALE)
        for n in range(len(slots)):
            part = weights[:, n * BLOCK : (n + 1) * BLOCK]
            total = part if total is None else total + part
        term = jnp.dot(weights.astype(jnp.bfloat16), values, preferred_element_type=jnp.float32)
        out = term if out is None else out + term
    out = out / jnp.sum(total, axis=1, keepdims=True)
    att[:, pl.ds(pl.multiple_of(head * HEAD, HEAD), HEAD)] = out.astype(jnp.bfloat16)


def remote(src, dst, send, recv, where):
    return pltpu.make_async_remote_copy(
        src_ref=src, dst_ref=dst, send_sem=send, recv_sem=recv, device_id=where, device_id_type=MESH
    )


def gather(k_hbm, v_hbm, kv, sems, core, y, z, up_y, down_y, up_z, down_z, twin, between):
    full_sem, half_sem, send_sem, twin_send, twin_recv, own_sem = sems

    def at_key(dy, dz):
        return key_slot(core, (y + dy + NY) % NY, (z + dz + NZ) % NZ)

    def at_value(dy, dz):
        return value_slot(core, (y + dy + NY) % NY, (z + dz + NZ) % NZ)

    def sem_of(slot):
        return slot % HALF + (slot // NB) * HALF

    def send(slot, where, half=None, source=None):
        source = kv.at[slot] if source is None else source
        target = kv.at[slot]
        if half is not None:
            source = source.at[pl.ds(half * 64, 64)]
            target = target.at[pl.ds(half * 64, 64)]
        recv = half_sem.at[sem_of(slot)] if half == 1 else full_sem.at[sem_of(slot)]
        remote(source, target, send_sem, recv, where).start()


    def pass_twin(slot, kind, source=None):
        source = kv.at[slot] if source is None else source
        remote(source, kv.at[slot], twin_send.at[kind], twin_recv.at[kind], twin).start()

    def arrived(slot, halves=False):
        if halves:
            for half, sem in ((0, full_sem), (1, half_sem)):
                piece = kv.at[slot].at[pl.ds(half * 64, 64)]
                pltpu.make_async_copy(piece, piece, sem.at[sem_of(slot)]).wait()
        else:
            pltpu.make_async_copy(kv.at[slot], kv.at[slot], full_sem.at[sem_of(slot)]).wait()

    mine_k, mine_v = at_key(0, 0), at_value(0, 0)
    for where in (up_z, down_z, up_y, down_y):
        send(mine_v, where, source=v_hbm)
        send(mine_k, where, source=k_hbm)
    pass_twin(mine_k, 0, k_hbm)
    pass_twin(mine_v, 1, v_hbm)
    between()

    events = []

    def key_column(dy):
        slot = at_key(dy, 0)
        send(slot, up_z)
        send(slot, down_z)
        pass_twin(slot, 0)

    def key_y_near():
        arrived(at_key(-1, 0))
        send(at_key(-1, 0), up_y, half=0)
        key_column(-1)
        arrived(at_key(1, 0))
        send(at_key(1, 0), down_y, half=1)
        key_column(1)

    def key_y_far():
        arrived(at_key(2, 0), halves=True)
        key_column(2)

    def key_z(dy, dz):
        for sign, where in ((-1, up_z), (1, down_z)):
            slot = at_key(dy, sign * dz)
            if dz == 4 and sign == 1:
                continue
            arrived(slot)
            if dz < 3 or (dz == 3 and (dy in (0, -1)) == (sign == -1)):
                send(slot, where)
            pass_twin(slot, 0)

    def value_row(dz):
        slot = at_value(0, dz)
        send(slot, up_y)
        send(slot, down_y)
        pass_twin(slot, 1)

    def value_z(dz):
        if dz == 4:
            arrived(at_value(0, 4), halves=True)
            value_row(4)
            return
        for sign, where, half in ((-1, up_z, 0), (1, down_z, 1)):
            slot = at_value(0, sign * dz)
            arrived(slot)
            if dz < 3:
                send(slot, where)
            else:
                send(slot, where, half=half)
            value_row(sign * dz)

    def value_y_near(dz):
        for sign, where in ((-1, up_y), (1, down_y)):
            slot = at_value(sign, dz)
            arrived(slot)
            if (dz <= 0) == (sign == -1):
                send(slot, where)
            pass_twin(slot, 1)

    def value_y_far(dz):
        slot = at_value(2, dz)
        arrived(slot)
        pass_twin(slot, 1)

    events.append((1, 0, lambda: value_z(1)))
    events.append((1, 1, key_y_near))
    events.append((2, 1, key_y_far))
    for d in (2, 3, 4):
        events.append((d, 0, lambda d=d: value_z(d)))
    for dy, base in ((0, 0), (-1, 1), (1, 1), (2, 2)):
        for d in (1, 2, 3, 4):
            events.append((base + d, 2, lambda dy=dy, d=d: key_z(dy, d)))
    for dz in (0, -1, 1, -2, 2, -3, 3, 4):
        events.append((abs(dz) + 1, 3, lambda dz=dz: value_y_near(dz)))
        events.append((abs(dz) + 2, 4, lambda dz=dz: value_y_far(dz)))
    for _, _, handler in sorted(events, key=lambda e: e[:2]):
        handler()

    other = (1 - core) * HALF
    for kind, base in ((0, 0), (1, NB)):
        half = kv.at[pl.ds(base + other, HALF)]
        pltpu.make_async_copy(half, half, twin_recv.at[kind]).wait()
        pltpu.make_async_copy(half, half, twin_send.at[kind]).wait()
    sent = kv.at[pl.ds(0, 62)]
    pltpu.make_async_copy(sent, sent, send_sem).wait()


def kernel(
    vert_ref, count_ref, slash_ref, q_hbm, k_hbm, v_hbm, w_hbm, out_ref,
    kv, q_vm, w_vm, scores, att, part, opp_in, dir_in, sum_in, sum_out,
    key_at, value_at, bias_at,
    full_sem, half_sem, send_sem, twin_send, twin_recv, own_sem, q_sem, w_sem,
    opp_sem, dir_sem, sum_sem, first_send, second_send,
):
    me, tp = lax.axis_index("seq"), lax.axis_index("tp")
    core, z, y = me % 2, (me // 2) % NZ, me // (2 * NZ)

    def seq_at(core, y, z):
        return {"seq": ((y + NY) % NY * NZ + (z + NZ) % NZ) * 2 + core}

    up_y, down_y = seq_at(core, y + 1, z), seq_at(core, y - 1, z)
    up_z, down_z = seq_at(core, y, z + 1), seq_at(core, y, z - 1)
    twin = seq_at(1 - core, y, z)
    right, left = {"tp": (tp + 1) % 4}, {"tp": (tp + 3) % 4}

    own_key, own_value = key_slot(core, y, z), value_slot(core, y, z)
    own_copies = [
        pltpu.make_async_copy(k_hbm, kv.at[own_key], own_sem.at[0]),
        pltpu.make_async_copy(v_hbm, kv.at[own_value], own_sem.at[1]),
    ]
    for copy in own_copies:
        copy.start()

    barrier = pltpu.get_barrier_semaphore()
    neighbours = (up_y, down_y, up_z, down_z, twin, right, left)
    for where in neighbours:
        pl.semaphore_signal(barrier, inc=1, device_id=where, device_id_type=MESH)
    pl.semaphore_wait(barrier, len(neighbours))

    def between():
        for head in range(HEADS):
            pltpu.make_async_copy(
                q_hbm.at[:, pl.ds(head * HEAD, HEAD)], q_vm.at[head], q_sem
            ).start()
        for p in range(PIECES):
            pltpu.make_async_copy(
                w_hbm.at[:, pl.ds(p * PIECE, PIECE)], w_vm.at[p], w_sem.at[p]
            ).start()

        @pl.loop(0, HEADS)
        def _(head):
            choose_blocks(head, me, vert_ref, count_ref, slash_ref, key_at, value_at, bias_at)

    gather(
        k_hbm, v_hbm, kv,
        (full_sem, half_sem, send_sem, twin_send, twin_recv, own_sem),
        core, y, z, up_y, down_y, up_z, down_z, twin, between,
    )
    for copy in own_copies:
        copy.wait()
    pltpu.make_async_copy(q_vm, q_vm, q_sem).wait()

    @pl.loop(0, HEADS // 2)
    def _(pair):
        for n in range(2):
            attend_head(
                pair * 2 + n, q_vm, kv, key_at, value_at, bias_at,
                own_key, own_value, scores.at[n], att,
            )

    def rows_of(p, target):
        return part.at[p, pl.ds(pl.multiple_of((target + 4) % 4 * ROWS, ROWS), ROWS)]

    @pl.loop(0, SIDE)
    def _(j):
        for p, ahead, behind, step in ((j, right, left, 1), (j + SIDE, left, right, -1)):
            pltpu.make_async_copy(w_vm.at[p], w_vm.at[p], w_sem.at[p]).wait()
            part[p] = jnp.dot(att[...], w_vm[p], preferred_element_type=jnp.float32).astype(
                jnp.bfloat16
            )
            remote(rows_of(p, tp + 2), opp_in.at[p], first_send, opp_sem.at[p], ahead).start()
            remote(rows_of(p, tp - step), dir_in.at[p], first_send, dir_sem.at[p], behind).start()

    @pl.loop(0, SIDE)
    def _(j):
        for p, ahead, step in ((j, right, 1), (j + SIDE, left, -1)):
            pltpu.make_async_copy(opp_in.at[p], opp_in.at[p], opp_sem.at[p]).wait()
            summed = opp_in[p].astype(jnp.float32) + rows_of(p, tp + step)[...].astype(jnp.float32)
            sum_out[p] = summed.astype(jnp.bfloat16)
            remote(sum_out.at[p], sum_in.at[p], second_send, sum_sem.at[p], ahead).start()

    for j in range(SIDE):
        for p in (j, j + SIDE):
            pltpu.make_async_copy(dir_in.at[p], dir_in.at[p], dir_sem.at[p]).wait()
            pltpu.make_async_copy(sum_in.at[p], sum_in.at[p], sum_sem.at[p]).wait()
            whole = (
                rows_of(p, tp)[...].astype(jnp.float32)
                + dir_in[p].astype(jnp.float32)
                + sum_in[p].astype(jnp.float32)
            )
            out_ref[:, p * PIECE : (p + 1) * PIECE] = whole.astype(jnp.bfloat16)
    pltpu.make_async_copy(part.at[pl.ds(0, SIDE)], part.at[pl.ds(0, SIDE)], first_send).wait()
    pltpu.make_async_copy(sum_out, sum_out, second_send).wait()


def body(queries, key_vectors, value_vectors, vertical, vertical_count, slash_offsets, out_weight):
    smem = pl.BlockSpec(memory_space=pltpu.SMEM)
    anywhere = pl.BlockSpec(memory_space=pl.ANY)
    bf16, dma = jnp.bfloat16, pltpu.SemaphoreType.DMA
    return pl.pallas_call(
        kernel,
        out_shape=jax.ShapeDtypeStruct((ROWS, D), bf16),
        in_specs=[smem] * 3 + [anywhere] * 4,
        out_specs=pl.BlockSpec(memory_space=pltpu.VMEM),
        scratch_shapes=[
            pltpu.VMEM((2 * NB, BLOCK, HEAD), bf16),
            pltpu.VMEM((HEADS, BLOCK, HEAD), bf16),
            pltpu.VMEM((PIECES, FEATURES, PIECE), bf16),
            pltpu.VMEM((2, BLOCK, SLOTS * BLOCK), jnp.float32),
            pltpu.VMEM((BLOCK, FEATURES), bf16),
            pltpu.VMEM((PIECES, BLOCK, PIECE), bf16),
            pltpu.VMEM((PIECES, ROWS, PIECE), bf16),
            pltpu.VMEM((PIECES, ROWS, PIECE), bf16),
            pltpu.VMEM((PIECES, ROWS, PIECE), bf16),
            pltpu.VMEM((PIECES, ROWS, PIECE), bf16),
            pltpu.SMEM((HEADS, 32), jnp.int32),
            pltpu.SMEM((HEADS, 32), jnp.int32),
            pltpu.SMEM((HEADS, 32), jnp.float32),
            dma((NB,)),
            dma((NB,)),
            dma,
            dma((2,)),
            dma((2,)),
            dma((2,)),
            dma,
            dma((PIECES,)),
            dma((PIECES,)),
            dma((PIECES,)),
            dma((PIECES,)),
            dma,
            dma,
        ],
        compiler_params=pltpu.CompilerParams(
            collective_id=0, has_side_effects=True, vmem_limit_bytes=48 * 1024 * 1024
        ),
        cost_estimate=pl.CostEstimate(
            flops=3_200_000_000, bytes_accessed=16_000_000, transcendentals=3_300_000
        ),
        name="attend_project",
    )(vertical, vertical_count, slash_offsets, queries, key_vectors, value_vectors, out_weight)


def solution(mesh):
    in_specs = (
        P("seq", "tp"),
        P("seq", "tp"),
        P("seq", "tp"),
        P("tp", None),
        P("tp"),
        P("tp", None),
        P("tp", None),
    )
    out_specs = P(("seq", "tp"), None)
    return jax.shard_map(body, mesh=mesh, in_specs=in_specs, out_specs=out_specs, check_vma=False)
```

time: 627 us -> 62.1 us (0.10)
  the two profiles are of different devices: /device:TPU:24 before, /device:TPU:1 now
where the time goes in v1:
time: 62.1 us; the launch traced here: 61.8 us
  Pallas kernels  56.6 us (91%)
  local copies, waits for them, and re-layouts  5.22 us (8%)
    pallas_call x1, Pallas kernels, body(): pl.pallas_call(kernel, out_shape=jax.ShapeDtypeStruct((ROWS, D), bf16), i...  56.6 us
    unnamed x13, local copies, waits for them, and re-layouts  5.22 us

profile of v1, /device:TPU:1, one launch (start us, length us, event | category | flops | bytes accessed | tf_op | source)
XLA Modules:
  0.0 61.8 jit_solution(16140970643405524762)
XLA Ops:
  0.0 0.0 copy-start
  0.0 0.9 %copy-done = bf16[128,1024]{1,0:T(8,128)(2,1)S(1)} copy-done((bf16[128,1024]{1,0:T(8,128)(2,1)S(1)}, bf16[128,1024]{1,0:T(8,128)(2,1)}, u32[]{:S(2)}) %copy-start) | copy-done | bytes 262168
  1.0 0.0 copy-start.1
  1.0 0.8 %copy-done.1 = bf16[128,128]{1,0:T(8,128)(2,1)S(1)} copy-done((bf16[128,128]{1,0:T(8,128)(2,1)S(1)}, bf16[128,128]{1,0:T(8,128)(2,1)}, u32[]{:S(2)}) %copy-start.1) | copy-done | bytes 32792
  1.7 0.0 copy-start.2
  1.7 0.8 %copy-done.2 = bf16[128,128]{1,0:T(8,128)(2,1)S(1)} copy-done((bf16[128,128]{1,0:T(8,128)(2,1)S(1)}, bf16[128,128]{1,0:T(8,128)(2,1)}, u32[]{:S(2)}) %copy-start.2) | copy-done | bytes 32792
  2.5 0.0 copy-start.3
  2.5 0.7 %copy-done.3 = s32[8,16]{1,0:T(8,128)S(1)} copy-done((s32[8,16]{1,0:T(8,128)S(1)}, s32[8,16]{1,0:T(8,128)}, u32[]{:S(2)}) %copy-start.3) | copy-done | bytes 536
  3.2 0.0 copy-start.4
  3.2 0.7 %copy-done.4 = s32[8,8]{1,0:T(8,128)S(1)} copy-done((s32[8,8]{1,0:T(8,128)S(1)}, s32[8,8]{1,0:T(8,128)}, u32[]{:S(2)}) %copy-start.4) | copy-done | bytes 280
  3.8 0.0 copy-start.5
  3.8 0.7 %copy-done.5 = s32[8]{0:T(128)S(1)} copy-done((s32[8]{0:T(128)S(1)}, s32[8]{0:T(128)}, u32[]{:S(2)}) %copy-start.5) | copy-done | bytes 56
  4.5 56.6 %attend_project.1 = bf16[32,5120]{1,0:T(8,128)(2,1)S(1)} custom-call(s32[8,16]{1,0:T(8,128)S(1)} %copy-done.3, s32[8]{0:T(128)S(1)} %copy-done.5, s32[8,8]{1,0:T(8,128)S(1)} %copy-done.4, bf16[128,1024]{1,0:T(8,128)(2,1)S(1)} %copy-done, bf16[128,128]{1,0:T(8,128)(2,1)S(1)} %copy-done.1, bf16[128,128]{1,0:T(8,128)(2,1)S(1)} %copy-done.2, ...), custom_call_target="tpu_custom_call" | custom-call | flops 3200000000 | bytes 16000000 | tf_op jit(solution)/shard_map/attend_project/pallas_call | solution.py:336
  61.1 0.7 %copy.9 = bf16[32,5120]{1,0:T(8,128)(2,1)} copy(bf16[32,5120]{1,0:T(8,128)(2,1)S(1)} %attend_project.1) | data formatting | bytes 655360
Async XLA Ops:
  0.0 0.9 %copy-start = (bf16[128,1024]{1,0:T(8,128)(2,1)S(1)}, bf16[128,1024]{1,0:T(8,128)(2,1)}, u32[]{:S(2)}) copy-start(bf16[128,1024]{1,0:T(8,128)(2,1)} %q_hbm.1) | copy-start | bytes 786436
  1.0 0.8 %copy-start.1 = (bf16[128,128]{1,0:T(8,128)(2,1)S(1)}, bf16[128,128]{1,0:T(8,128)(2,1)}, u32[]{:S(2)}) copy-start(bf16[128,128]{1,0:T(8,128)(2,1)} %k_hbm.1) | copy-start | bytes 98308
  1.7 0.8 %copy-start.2 = (bf16[128,128]{1,0:T(8,128)(2,1)S(1)}, bf16[128,128]{1,0:T(8,128)(2,1)}, u32[]{:S(2)}) copy-start(bf16[128,128]{1,0:T(8,128)(2,1)} %v_hbm.1) | copy-start | bytes 98308
  2.5 0.7 %copy-start.3 = (s32[8,16]{1,0:T(8,128)S(1)}, s32[8,16]{1,0:T(8,128)}, u32[]{:S(2)}) copy-start(s32[8,16]{1,0:T(8,128)} %vert_ref.1) | copy-start | bytes 1540
  3.2 0.7 %copy-start.4 = (s32[8,8]{1,0:T(8,128)S(1)}, s32[8,8]{1,0:T(8,128)}, u32[]{:S(2)}) copy-start(s32[8,8]{1,0:T(8,128)} %slash_ref.1) | copy-start | bytes 772
  3.8 0.7 %copy-start.5 = (s32[8]{0:T(128)S(1)}, s32[8]{0:T(128)}, u32[]{:S(2)}) copy-start(s32[8]{0:T(128)} %count_ref.1) | copy-start | bytes 100

commit v2 on v1

v2 whole, which is shorter than its diff:
```python
import functools
import math

import jax
import jax.numpy as jnp
from jax import lax
from jax.experimental import pallas as pl
from jax.experimental.pallas import tpu as pltpu
from jax.sharding import PartitionSpec as P

HEAD = 128
BLOCK = 128
HEADS = 8
NY, NZ = 4, 8
NB = 64
HALF = NB // 2
NSLASH, NVERT = 8, 16
SLOTS = 1 + NSLASH + NVERT
D = 5120
PIECE = 512
SIDE = D // PIECE // 2
PIECES = 2 * SIDE
ROWS = 32
FEATURES = HEADS * HEAD
EXP2_SCALE = HEAD**-0.5 * math.log2(math.e)
MESH = pl.DeviceIdType.MESH
NEG = float("-inf")


def key_slot(core, y, z):
    return core * HALF + z * NY + y


def value_slot(core, y, z):
    return core * HALF + y * NZ + z


def choose_blocks(head, me, vert_ref, count_ref, slash_ref, key_at, value_at, bias_at):
    low = jnp.where(me < 32, jnp.left_shift(jnp.int32(1), me % 32), 0)
    high = jnp.where(me < 32, 0, jnp.left_shift(jnp.int32(1), me % 32))
    count = count_ref[head]
    for c in range(1, SLOTS):
        if c <= NSLASH:
            block = me - slash_ref[head, c - 1]
            usable = block >= 0
        else:
            block = vert_ref[head, c - 1 - NSLASH]
            usable = (block <= me) & (c - 1 - NSLASH < count)
        block = jnp.clip(block, 0, NB - 1)
        bit = jnp.left_shift(jnp.int32(1), block % 32)
        in_low = block < 32
        seen = (jnp.where(in_low, low, high) & bit) != 0
        kept = usable & jnp.logical_not(seen)
        add = jnp.where(kept, bit, 0)
        low = low | jnp.where(in_low, add, 0)
        high = high | jnp.where(in_low, 0, add)
        core, z, y = block % 2, (block // 2) % NZ, block // (2 * NZ)
        key_at[head, c] = key_slot(core, y, z)
        value_at[head, c] = value_slot(core, y, z)
        bias_at[head, c] = jnp.where(kept, jnp.float32(0), jnp.float32(NEG))


def slot_groups(size):
    return [list(range(c, min(c + size, SLOTS))) for c in range(0, SLOTS, size)]


def weigh_head(head, q_vm, keys_vm, key_at, bias_at, own_key, scores, weights, scale_by):
    query = q_vm[head]
    rows = lax.broadcasted_iota(jnp.int32, (BLOCK, BLOCK), 0)
    cols = lax.broadcasted_iota(jnp.int32, (BLOCK, BLOCK), 1)
    top = None
    for slots in slot_groups(2):
        keys = [keys_vm[own_key if s == 0 else key_at[head, s]] for s in slots]
        keys = keys[0] if len(keys) == 1 else jnp.concatenate(keys, axis=0)
        both = lax.dot_general(
            query, keys, (((1,), (1,)), ((), ())), preferred_element_type=jnp.float32
        )
        for n, s in enumerate(slots):
            part = both[:, n * BLOCK : (n + 1) * BLOCK]
            if s == 0:
                part = jnp.where(cols <= rows, part, NEG)
            else:
                part = part + bias_at[head, s]
            scores[:, s * BLOCK : (s + 1) * BLOCK] = part
            top = part if top is None else jnp.maximum(top, part)
    top = jnp.max(top, axis=1, keepdims=True)
    total = None
    for s in range(SLOTS):
        at = slice(s * BLOCK, (s + 1) * BLOCK)
        part = jnp.exp2((scores[:, at] - top) * EXP2_SCALE)
        weights[head, :, at] = part.astype(jnp.bfloat16)
        total = part if total is None else total + part
    total = jnp.sum(total, axis=1, keepdims=True)
    scale_by[head] = jnp.broadcast_to(1.0 / total, (BLOCK, HEAD))


def combine_head(head, values_vm, value_at, own_value, weights, scale_by, att):
    out = None
    for slots in slot_groups(4):
        values = [values_vm[own_value if s == 0 else value_at[head, s]] for s in slots]
        values = values[0] if len(values) == 1 else jnp.concatenate(values, axis=0)
        part = weights[head, :, slots[0] * BLOCK : (slots[-1] + 1) * BLOCK]
        term = jnp.dot(part, values, preferred_element_type=jnp.float32)
        out = term if out is None else out + term
    out = out * scale_by[head]
    att[:, pl.ds(pl.multiple_of(head * HEAD, HEAD), HEAD)] = out.astype(jnp.bfloat16)


def remote(src, dst, send, recv, where):
    return pltpu.make_async_remote_copy(
        src_ref=src, dst_ref=dst, send_sem=send, recv_sem=recv, device_id=where, device_id_type=MESH
    )


class Gather:
    def __init__(self, buffers, sems, sources, core, y, z, seq_at):
        self.buffers, self.sources, self.core, self.y, self.z = buffers, sources, core, y, z
        self.full_sem, self.half_sem, self.send_sem, self.twin_send, self.twin_recv = sems
        self.up_y, self.down_y = seq_at(core, y + 1, z), seq_at(core, y - 1, z)
        self.far_y = seq_at(core, y + 2, z)
        self.along = {d: seq_at(core, y, z + d) for d in (-2, -1, 1, 2)}
        self.twin = seq_at(1 - core, y, z)

    def slot(self, kind, dy, dz):
        at = key_slot if kind == 0 else value_slot
        return at(self.core, (self.y + dy + NY) % NY, (self.z + dz + NZ) % NZ)

    def send(self, kind, slot, where, half=None, source=None):
        target = self.buffers[kind].at[slot]
        source = target if source is None else source
        if half is not None:
            source = source.at[pl.ds(half * 64, 64)]
            target = target.at[pl.ds(half * 64, 64)]
        recv = (self.half_sem if half == 1 else self.full_sem).at[kind, slot % HALF]
        remote(source, target, self.send_sem.at[kind], recv, where).start()

    def to_twin(self, kind, slot, source=None):
        target = self.buffers[kind].at[slot]
        source = target if source is None else source
        send, recv = self.twin_send.at[kind], self.twin_recv.at[kind]
        remote(source, target, send, recv, self.twin).start()

    def arrived(self, kind, slot, halves=False):
        whole = self.buffers[kind].at[slot]
        if halves:
            for half, sem in ((0, self.full_sem), (1, self.half_sem)):
                piece = whole.at[pl.ds(half * 64, 64)]
                pltpu.make_async_copy(piece, piece, sem.at[kind, slot % HALF]).wait()
        else:
            pltpu.make_async_copy(whole, whole, self.full_sem.at[kind, slot % HALF]).wait()

    def start(self, kind):
        source, slot = self.sources[kind], self.slot(kind, 0, 0)
        self.send(kind, slot, self.far_y, source=source)
        for d in (2, -2, 1, -1):
            self.send(kind, slot, self.along[d], source=source)
        for where in (self.up_y, self.down_y):
            self.send(kind, slot, where, source=source)
        self.to_twin(kind, slot, source)

    def sideways(self, kind, slot):
        self.send(kind, slot, self.up_y)
        self.send(kind, slot, self.down_y)

    def onward(self, kind, slot, sign):
        self.send(kind, slot, self.along[sign])
        self.send(kind, slot, self.along[2 * sign], half=0 if sign == 1 else 1)

    def near(self, kind):
        slot = self.slot(kind, 2, 0)
        self.arrived(kind, slot)
        for d in (2, -2, 1, -1):
            self.send(kind, slot, self.along[d])
        self.to_twin(kind, slot)
        for sign in (1, -1):
            slot = self.slot(kind, 0, -2 * sign)
            self.arrived(kind, slot)
            self.onward(kind, slot, sign)
            self.sideways(kind, slot)
            self.to_twin(kind, slot)
        for sign in (1, -1):
            slot = self.slot(kind, 0, -sign)
            self.arrived(kind, slot)
            self.sideways(kind, slot)
            self.to_twin(kind, slot)

    def middle(self, kind):
        for sign in (1, -1):
            slot = self.slot(kind, 0, -3 * sign)
            self.arrived(kind, slot)
            self.sideways(kind, slot)
            self.to_twin(kind, slot)
        slot = self.slot(kind, 0, 4)
        self.arrived(kind, slot, halves=True)
        self.sideways(kind, slot)
        self.to_twin(kind, slot)
        for sign in (1, -1):
            slot = self.slot(kind, 2, -2 * sign)
            self.arrived(kind, slot)
            self.onward(kind, slot, sign)
            self.to_twin(kind, slot)

    def last(self, kind):
        todo = []
        for dz in (0, 1, -1, 2, -2):
            todo += [(1, dz, False), (-1, dz, False)]
        todo += [(2, 1, False), (2, -1, False)]
        for dz in (3, -3):
            todo += [(1, dz, False), (-1, dz, False), (2, dz, False)]
        todo += [(1, 4, False), (-1, 4, False), (2, 4, True)]

        def one(dy, dz, halves):
            slot = self.slot(kind, dy, dz)
            self.arrived(kind, slot, halves)
            self.to_twin(kind, slot)

        return [functools.partial(one, *t) for t in todo]

    def other_half(self, kind):
        half = self.buffers[kind].at[pl.ds((1 - self.core) * HALF, HALF)]
        pltpu.make_async_copy(half, half, self.twin_recv.at[kind]).wait()

    def sent(self):
        for kind, buffer in enumerate(self.buffers):
            half, every = buffer.at[pl.ds(0, HALF)], buffer.at[pl.ds(0, HALF - 1)]
            pltpu.make_async_copy(half, half, self.twin_send.at[kind]).wait()
            pltpu.make_async_copy(every, every, self.send_sem.at[kind]).wait()


def kernel(
    vert_hbm, count_hbm, slash_hbm, q_hbm, k_hbm, v_hbm, w_hbm, out_hbm,
    keys_vm, values_vm, q_vm, w_vm, scores, weights, scale_by, att, part,
    opp_in, dir_in, sum_in, sum_out, out_vm,
    vert_ref, count_ref, slash_ref, key_at, value_at, bias_at,
    full_sem, half_sem, send_sem, twin_send, twin_recv, own_sem, q_sem, w_sem, out_sem,
    opp_sem, dir_sem, sum_sem, first_send, second_send,
):
    me, tp = lax.axis_index("seq"), lax.axis_index("tp")
    core, z, y = me % 2, (me // 2) % NZ, me // (2 * NZ)

    def seq_at(core, y, z):
        return {"seq": ((y + NY) % NY * NZ + (z + NZ) % NZ) * 2 + core}

    right, left = {"tp": (tp + 1) % 4}, {"tp": (tp + 3) % 4}
    own_key, own_value = key_slot(core, y, z), value_slot(core, y, z)
    own_copies = [
        pltpu.make_async_copy(source, target, own_sem.at[n])
        for n, (source, target) in enumerate(
            (
                (k_hbm, keys_vm.at[own_key]),
                (v_hbm, values_vm.at[own_value]),
                (vert_hbm, vert_ref),
                (count_hbm, count_ref),
                (slash_hbm, slash_ref),
            )
        )
    ]
    for copy in own_copies:
        copy.start()
    for head in range(HEADS):
        pltpu.make_async_copy(
            q_hbm.at[:, pl.ds(head * HEAD, HEAD)], q_vm.at[head], q_sem
        ).start()
    for p in range(PIECES):
        pltpu.make_async_copy(
            w_hbm.at[:, pl.ds(p * PIECE, PIECE)], w_vm.at[p], w_sem.at[p]
        ).start()

    moves = Gather(
        (keys_vm, values_vm), (full_sem, half_sem, send_sem, twin_send, twin_recv),
        (k_hbm, v_hbm), core, y, z, seq_at,
    )
    barrier = pltpu.get_barrier_semaphore()
    neighbours = (
        moves.up_y, moves.down_y, moves.far_y, moves.twin, right, left, *moves.along.values()
    )
    for where in neighbours:
        pl.semaphore_signal(barrier, inc=1, device_id=where, device_id_type=MESH)
    pl.semaphore_wait(barrier, len(neighbours))

    moves.start(0)
    moves.start(1)
    for copy in own_copies:
        copy.wait()

    @pl.loop(0, HEADS)
    def _(head):
        choose_blocks(head, me, vert_ref, count_ref, slash_ref, key_at, value_at, bias_at)

    moves.near(0)
    moves.near(1)
    moves.middle(0)
    moves.middle(1)
    for handler in moves.last(0):
        handler()
    pltpu.make_async_copy(q_vm, q_vm, q_sem).wait()
    moves.other_half(0)

    def weigh(head, n):
        weigh_head(
            head, q_vm, keys_vm, key_at, bias_at, own_key, scores.at[n], weights, scale_by
        )

    @pl.loop(0, HEADS // 4)
    def _(pair):
        weigh(pair * 2, 0)
        weigh(pair * 2 + 1, 1)

    handlers = moves.last(1)
    half_way = len(handlers) // 2
    for handler in handlers[:half_way]:
        handler()
    weigh(HEADS // 2, 0)
    weigh(HEADS // 2 + 1, 1)
    for handler in handlers[half_way:]:
        handler()
    weigh(HEADS // 2 + 2, 0)
    weigh(HEADS // 2 + 3, 1)
    moves.other_half(1)

    @pl.loop(0, HEADS // 2)
    def _(pair):
        for n in range(2):
            combine_head(pair * 2 + n, values_vm, value_at, own_value, weights, scale_by, att)

    def rows_of(p, target):
        return part.at[p, pl.ds(pl.multiple_of((target + 4) % 4 * ROWS, ROWS), ROWS)]

    @pl.loop(0, SIDE)
    def _(j):
        for p, ahead, behind, step in ((j, right, left, 1), (j + SIDE, left, right, -1)):
            pltpu.make_async_copy(w_vm.at[p], w_vm.at[p], w_sem.at[p]).wait()
            part[p] = jnp.dot(att[...], w_vm[p], preferred_element_type=jnp.float32).astype(
                jnp.bfloat16
            )
            remote(rows_of(p, tp + 2), opp_in.at[p], first_send, opp_sem.at[p], ahead).start()
            remote(rows_of(p, tp - step), dir_in.at[p], first_send, dir_sem.at[p], behind).start()

    @pl.loop(0, SIDE)
    def _(j):
        for p, ahead, step in ((j, right, 1), (j + SIDE, left, -1)):
            pltpu.make_async_copy(opp_in.at[p], opp_in.at[p], opp_sem.at[p]).wait()
            summed = opp_in[p].astype(jnp.float32) + rows_of(p, tp + step)[...].astype(jnp.float32)
            sum_out[p] = summed.astype(jnp.bfloat16)
            remote(sum_out.at[p], sum_in.at[p], second_send, sum_sem.at[p], ahead).start()

    for j in range(SIDE):
        for p in (j, j + SIDE):
            pltpu.make_async_copy(dir_in.at[p], dir_in.at[p], dir_sem.at[p]).wait()
            pltpu.make_async_copy(sum_in.at[p], sum_in.at[p], sum_sem.at[p]).wait()
            whole = (
                rows_of(p, tp)[...].astype(jnp.float32)
                + dir_in[p].astype(jnp.float32)
                + sum_in[p].astype(jnp.float32)
            )
            at = slice(p * PIECE, (p + 1) * PIECE)
            out_vm[:, at] = whole.astype(jnp.bfloat16)
            pltpu.make_async_copy(out_vm.at[:, at], out_hbm.at[:, at], out_sem).start()
    pltpu.make_async_copy(part.at[pl.ds(0, SIDE)], part.at[pl.ds(0, SIDE)], first_send).wait()
    pltpu.make_async_copy(sum_out, sum_out, second_send).wait()
    moves.sent()
    pltpu.make_async_copy(out_vm, out_hbm, out_sem).wait()


def body(queries, key_vectors, value_vectors, vertical, vertical_count, slash_offsets, out_weight):
    anywhere = pl.BlockSpec(memory_space=pl.ANY)
    bf16, dma = jnp.bfloat16, pltpu.SemaphoreType.DMA
    return pl.pallas_call(
        kernel,
        out_shape=jax.ShapeDtypeStruct((ROWS, D), bf16),
        in_specs=[anywhere] * 7,
        out_specs=anywhere,
        scratch_shapes=[
            pltpu.VMEM((NB, BLOCK, HEAD), bf16),
            pltpu.VMEM((NB, BLOCK, HEAD), bf16),
            pltpu.VMEM((HEADS, BLOCK, HEAD), bf16),
            pltpu.VMEM((PIECES, FEATURES, PIECE), bf16),
            pltpu.VMEM((2, BLOCK, SLOTS * BLOCK), jnp.float32),
            pltpu.VMEM((HEADS, BLOCK, SLOTS * BLOCK), bf16),
            pltpu.VMEM((HEADS, BLOCK, HEAD), jnp.float32),
            pltpu.VMEM((BLOCK, FEATURES), bf16),
            pltpu.VMEM((PIECES, BLOCK, PIECE), bf16),
            pltpu.VMEM((PIECES, ROWS, PIECE), bf16),
            pltpu.VMEM((PIECES, ROWS, PIECE), bf16),
            pltpu.VMEM((PIECES, ROWS, PIECE), bf16),
            pltpu.VMEM((PIECES, ROWS, PIECE), bf16),
            pltpu.VMEM((ROWS, D), bf16),
            pltpu.SMEM((HEADS, NVERT), jnp.int32),
            pltpu.SMEM((HEADS,), jnp.int32),
            pltpu.SMEM((HEADS, NSLASH), jnp.int32),
            pltpu.SMEM((HEADS, 32), jnp.int32),
            pltpu.SMEM((HEADS, 32), jnp.int32),
            pltpu.SMEM((HEADS, 32), jnp.float32),
            dma((2, HALF)),
            dma((2, HALF)),
            dma((2,)),
            dma((2,)),
            dma((2,)),
            dma((5,)),
            dma,
            dma((PIECES,)),
            dma,
            dma((PIECES,)),
            dma((PIECES,)),
            dma((PIECES,)),
            dma,
            dma,
        ],
        compiler_params=pltpu.CompilerParams(
            collective_id=0, has_side_effects=True, vmem_limit_bytes=64 * 1024 * 1024
        ),
        cost_estimate=pl.CostEstimate(
            flops=3_200_000_000, bytes_accessed=16_000_000, transcendentals=3_300_000
        ),
        name="attend_project",
    )(vertical, vertical_count, slash_offsets, queries, key_vectors, value_vectors, out_weight)


def solution(mesh):
    in_specs = (
        P("seq", "tp"),
        P("seq", "tp"),
        P("seq", "tp"),
        P("tp", None),
        P("tp"),
        P("tp", None),
        P("tp", None),
    )
    out_specs = P(("seq", "tp"), None)
    return jax.shard_map(body, mesh=mesh, in_specs=in_specs, out_specs=out_specs, check_vma=False)
```

time: 62.1 us -> 50.4 us (0.81)
  Pallas kernels: 56.6 us -> 48.5 us
  local copies, waits for them, and re-layouts: 5.22 us -> 1.72 us
    pallas_call x1, Pallas kernels: 56.6 us -> 48.5 us  [body(): pl.pallas_call(kernel, out_shape=jax.ShapeDtypeStruct((ROWS, D), bf16), i...]
    unnamed x13 -> x1, local copies, waits for them, and re-layouts: 5.22 us -> 1.72 us
where the time goes in v2:
time: 50.4 us; the launch traced here: 50.3 us
  Pallas kernels  48.5 us (96%)
  local copies, waits for them, and re-layouts  1.72 us (3%)
    pallas_call x1, Pallas kernels, body(): pl.pallas_call(kernel, out_shape=jax.ShapeDtypeStruct((ROWS, D), bf16), i...  48.5 us
    unnamed x1, local copies, waits for them, and re-layouts  1.72 us

profile of v2, /device:TPU:1, one launch (start us, length us, event | category | flops | bytes accessed | tf_op | source)
XLA Modules:
  0.0 50.3 jit_solution(11816881835842411730)
XLA Ops:
  0.0 48.5 %attend_project.1 = bf16[32,5120]{1,0:T(8,128)(2,1)} custom-call(s32[8,16]{1,0:T(8,128)} %vert_hbm.1, s32[8]{0:T(128)} %count_hbm.1, s32[8,8]{1,0:T(8,128)} %slash_hbm.1, bf16[128,1024]{1,0:T(8,128)(2,1)} %q_hbm.1, bf16[128,128]{1,0:T(8,128)(2,1)} %k_hbm.1, bf16[128,128]{1,0:T(8,128)(2,1)} %v_hbm.1, bf16[1024,5120]{1,0:T(8,128)(2,1)} %w_hbm.1), custom_call_target="tpu_custom_call" | custom-call | flops 3200000000 | bytes 16000000 | tf_op jit(solution)/shard_map/attend_project/pallas_call | solution.py:368
  48.5 1.7 %copy.9 = bf16[32,5120]{1,0:T(8,128)(2,1)} copy(bf16[32,5120]{1,0:T(8,128)(2,1)} %attend_project.1) | data formatting | bytes 655360

commit v3 on v2

--- a/solution.py
+++ b/solution.py
@@ -24,6 +24,10 @@
 FEATURES = HEADS * HEAD
 EXP2_SCALE = HEAD**-0.5 * math.log2(math.e)
 MESH = pl.DeviceIdType.MESH
+CUTS = (0, 2, 4, 6)
+ROW_BLOCKS = tuple(NZ * (row + 1) for row in range(NY))
+SENT = (24, 16, 22, 14)
+HOPS_Z = (0, 1, 1, 2, 2)
 NEG = float("-inf")
 
 
@@ -46,7 +50,7 @@
         else:
             block = vert_ref[head, c - 1 - NSLASH]
             usable = (block <= me) & (c - 1 - NSLASH < count)
-        block = jnp.clip(block, 0, NB - 1)
+        block = jnp.where(usable, block, me)
         bit = jnp.left_shift(jnp.int32(1), block % 32)
         in_low = block < 32
         seen = (jnp.where(in_low, low, high) & bit) != 0
@@ -116,14 +120,17 @@
     def __init__(self, buffers, sems, sources, core, y, z, seq_at):
         self.buffers, self.sources, self.core, self.y, self.z = buffers, sources, core, y, z
         self.full_sem, self.half_sem, self.send_sem, self.twin_send, self.twin_recv = sems
-        self.up_y, self.down_y = seq_at(core, y + 1, z), seq_at(core, y - 1, z)
-        self.far_y = seq_at(core, y + 2, z)
-        self.along = {d: seq_at(core, y, z + d) for d in (-2, -1, 1, 2)}
+        other = 1 - core
+        self.up_y, self.down_y = seq_at(other, y + 1, z), seq_at(other, y - 1, z)
+        self.far_y = seq_at(other, y + 2, z)
+        self.along = {d: seq_at(other, y, z + d) for d in (-2, -1, 1, 2)}
         self.twin = seq_at(1 - core, y, z)
 
     def slot(self, kind, dy, dz):
+        hops = HOPS_Z[abs(dz)] + (dy in (1, -1)) if abs(dy) < 2 else 1 + HOPS_Z[abs(dz)]
+        core = self.core if hops % 2 == 0 else 1 - self.core
         at = key_slot if kind == 0 else value_slot
-        return at(self.core, (self.y + dy + NY) % NY, (self.z + dz + NZ) % NZ)
+        return at(core, (self.y + dy + NY) % NY, (self.z + dz + NZ) % NZ)
 
     def send(self, kind, slot, where, half=None, source=None):
         target = self.buffers[kind].at[slot]
@@ -149,82 +156,103 @@
         else:
             pltpu.make_async_copy(whole, whole, self.full_sem.at[kind, slot % HALF]).wait()
 
-    def start(self, kind):
+    def beside(self, kind, slot, source=None):
+        @pl.when(self.y < NY - 1)
+        def _():
+            self.send(kind, slot, self.up_y, source=source)
+
+        @pl.when(self.y == 0)
+        def _():
+            self.send(kind, slot, self.down_y, source=source)
+
+    def own(self, kind):
         source, slot = self.sources[kind], self.slot(kind, 0, 0)
-        self.send(kind, slot, self.far_y, source=source)
+
+        @pl.when(self.y < 2)
+        def _():
+            self.send(kind, slot, self.far_y, source=source)
+
         for d in (2, -2, 1, -1):
             self.send(kind, slot, self.along[d], source=source)
-        for where in (self.up_y, self.down_y):
-            self.send(kind, slot, where, source=source)
+        self.beside(kind, slot, source)
         self.to_twin(kind, slot, source)
 
-    def sideways(self, kind, slot):
-        self.send(kind, slot, self.up_y)
-        self.send(kind, slot, self.down_y)
-
-    def onward(self, kind, slot, sign):
-        self.send(kind, slot, self.along[sign])
-        self.send(kind, slot, self.along[2 * sign], half=0 if sign == 1 else 1)
-
-    def near(self, kind):
-        slot = self.slot(kind, 2, 0)
-        self.arrived(kind, slot)
-        for d in (2, -2, 1, -1):
+    def take(self, kind, dy, dz, on=(), half_on=()):
+        slot = self.slot(kind, dy, dz)
+        self.arrived(kind, slot, halves=dz == 4 and dy in (0, 2))
+        for d in on:
             self.send(kind, slot, self.along[d])
+        for d in half_on:
+            self.send(kind, slot, self.along[d], half=0 if d > 0 else 1)
+        if dy == 0:
+            self.beside(kind, slot)
         self.to_twin(kind, slot)
-        for sign in (1, -1):
-            slot = self.slot(kind, 0, -2 * sign)
-            self.arrived(kind, slot)
-            self.onward(kind, slot, sign)
-            self.sideways(kind, slot)
-            self.to_twin(kind, slot)
-        for sign in (1, -1):
-            slot = self.slot(kind, 0, -sign)
-            self.arrived(kind, slot)
-            self.sideways(kind, slot)
-            self.to_twin(kind, slot)
-
-    def middle(self, kind):
-        for sign in (1, -1):
-            slot = self.slot(kind, 0, -3 * sign)
-            self.arrived(kind, slot)
-            self.sideways(kind, slot)
-            self.to_twin(kind, slot)
-        slot = self.slot(kind, 0, 4)
-        self.arrived(kind, slot, halves=True)
-        self.sideways(kind, slot)
-        self.to_twin(kind, slot)
-        for sign in (1, -1):
-            slot = self.slot(kind, 2, -2 * sign)
-            self.arrived(kind, slot)
-            self.onward(kind, slot, sign)
-            self.to_twin(kind, slot)
+
+    def when_far(self, *steps):
+        def run():
+            @pl.when(self.y >= 2)
+            def _():
+                for step in steps:
+                    step()
+
+        return run
+
+    def stages(self, kind):
+        take = functools.partial(self.take, kind)
+        first = [functools.partial(self.own, kind)]
+        near = [self.when_far(lambda: take(2, 0, (2, -2, 1, -1)))]
+        near += [lambda s=s: take(0, -2 * s, (s,), (2 * s,)) for s in (1, -1)]
+        near += [lambda s=s: take(0, -s) for s in (1, -1)]
+        middle = [self.when_far(*(lambda s=s: take(2, -2 * s, (s,), (2 * s,)) for s in (1, -1)))]
+        middle += [lambda s=s: take(0, -3 * s) for s in (1, -1)]
+        middle += [lambda: take(0, 4)]
+        return [first, near, middle, self.last(kind)]
 
     def last(self, kind):
-        todo = []
-        for dz in (0, 1, -1, 2, -2):
-            todo += [(1, dz, False), (-1, dz, False)]
-        todo += [(2, 1, False), (2, -1, False)]
-        for dz in (3, -3):
-            todo += [(1, dz, False), (-1, dz, False), (2, dz, False)]
-        todo += [(1, 4, False), (-1, 4, False), (2, 4, True)]
-
-        def one(dy, dz, halves):
-            slot = self.slot(kind, dy, dz)
-            self.arrived(kind, slot, halves)
-            self.to_twin(kind, slot)
-
-        return [functools.partial(one, *t) for t in todo]
+        take = functools.partial(self.take, kind)
+
+        def beside(*shifts):
+            def run():
+                @pl.when(self.y >= 1)
+                def _():
+                    for dz in shifts:
+                        take(-1, dz)
+
+                @pl.when(self.y == NY - 1)
+                def _():
+                    for dz in shifts:
+                        take(1, dz)
+
+            return run
+
+        return [
+            beside(0),
+            beside(1, -1),
+            self.when_far(lambda: take(2, 1), lambda: take(2, -1)),
+            beside(2),
+            beside(-2),
+            beside(3),
+            beside(-3),
+            self.when_far(lambda: take(2, 3), lambda: take(2, -3)),
+            beside(4),
+            self.when_far(lambda: take(2, 4)),
+        ]
+
+    def by_row(self, kind, sem, blocks):
+        for row, count in enumerate(blocks):
+
+            @pl.when(self.y == row)
+            def _(count=count):
+                due = self.buffers[kind].at[pl.ds(0, count)]
+                pltpu.make_async_copy(due, due, sem.at[kind]).wait()
 
     def other_half(self, kind):
-        half = self.buffers[kind].at[pl.ds((1 - self.core) * HALF, HALF)]
-        pltpu.make_async_copy(half, half, self.twin_recv.at[kind]).wait()
+        self.by_row(kind, self.twin_recv, ROW_BLOCKS)
 
     def sent(self):
-        for kind, buffer in enumerate(self.buffers):
-            half, every = buffer.at[pl.ds(0, HALF)], buffer.at[pl.ds(0, HALF - 1)]
-            pltpu.make_async_copy(half, half, self.twin_send.at[kind]).wait()
-            pltpu.make_async_copy(every, every, self.send_sem.at[kind]).wait()
+        for kind in (0, 1):
+            self.by_row(kind, self.twin_send, ROW_BLOCKS)
+            self.by_row(kind, self.send_sem, SENT)
 
 
 def kernel(
@@ -272,14 +300,20 @@
     )
     barrier = pltpu.get_barrier_semaphore()
     neighbours = (
-        moves.up_y, moves.down_y, moves.far_y, moves.twin, right, left, *moves.along.values()
+        moves.up_y, moves.down_y, moves.far_y, moves.twin, right, left, *moves.along.values(),
     )
     for where in neighbours:
         pl.semaphore_signal(barrier, inc=1, device_id=where, device_id_type=MESH)
     pl.semaphore_wait(barrier, len(neighbours))
 
-    moves.start(0)
-    moves.start(1)
+    keys, values = moves.stages(0), moves.stages(1)
+
+    def do(stage):
+        for handler in stage:
+            handler()
+
+    do(keys[0])
+    do(values[0])
     for copy in own_copies:
         copy.wait()
 
@@ -287,12 +321,8 @@
     def _(head):
         choose_blocks(head, me, vert_ref, count_ref, slash_ref, key_at, value_at, bias_at)
 
-    moves.near(0)
-    moves.near(1)
-    moves.middle(0)
-    moves.middle(1)
-    for handler in moves.last(0):
-        handler()
+    for stage in (keys[1], values[1], keys[2], values[2], keys[3]):
+        do(stage)
     pltpu.make_async_copy(q_vm, q_vm, q_sem).wait()
     moves.other_half(0)
 
@@ -301,21 +331,13 @@
             head, q_vm, keys_vm, key_at, bias_at, own_key, scores.at[n], weights, scale_by
         )
 
-    @pl.loop(0, HEADS // 4)
-    def _(pair):
-        weigh(pair * 2, 0)
-        weigh(pair * 2 + 1, 1)
-
-    handlers = moves.last(1)
-    half_way = len(handlers) // 2
-    for handler in handlers[:half_way]:
-        handler()
-    weigh(HEADS // 2, 0)
-    weigh(HEADS // 2 + 1, 1)
-    for handler in handlers[half_way:]:
-        handler()
-    weigh(HEADS // 2 + 2, 0)
-    weigh(HEADS // 2 + 3, 1)
+    ends = values[3]
+    cuts = [0] + [len(ends) * c // 8 for c in CUTS] + [len(ends)]
+    for n in range(HEADS // 2):
+        do(ends[cuts[n] : cuts[n + 1]])
+        weigh(2 * n, 0)
+        weigh(2 * n + 1, 1)
+    do(ends[cuts[HEADS // 2] :])
     moves.other_half(1)
 
     @pl.loop(0, HEADS // 2)

time: 50.4 us -> 50.1 us (level)
  the two profiles are of different devices: /device:TPU:1 before, /device:TPU:24 now
where the time goes in v3:
time: 50.1 us; the launch traced here: 49.5 us
  Pallas kernels  47.8 us (95%)
  local copies, waits for them, and re-layouts  1.72 us (3%)
    pallas_call x1, Pallas kernels, body(): pl.pallas_call(kernel, out_shape=jax.ShapeDtypeStruct((ROWS, D), bf16), i...  47.8 us
    unnamed x1, local copies, waits for them, and re-layouts  1.72 us

profile of v3, /device:TPU:24, one launch (start us, length us, event | category | flops | bytes accessed | tf_op | source)
XLA Modules:
  0.0 49.5 jit_solution(17005115460574312750)
XLA Ops:
  0.0 47.8 %attend_project.1 = bf16[32,5120]{1,0:T(8,128)(2,1)} custom-call(s32[8,16]{1,0:T(8,128)} %vert_hbm.1, s32[8]{0:T(128)} %count_hbm.1, s32[8,8]{1,0:T(8,128)} %slash_hbm.1, bf16[128,1024]{1,0:T(8,128)(2,1)} %q_hbm.1, bf16[128,128]{1,0:T(8,128)(2,1)} %k_hbm.1, bf16[128,128]{1,0:T(8,128)(2,1)} %v_hbm.1, bf16[1024,5120]{1,0:T(8,128)(2,1)} %w_hbm.1), custom_call_target="tpu_custom_call" | custom-call | flops 3200000000 | bytes 16000000 | tf_op jit(solution)/shard_map/attend_project/pallas_call | solution.py:390
  47.8 1.7 %copy.9 = bf16[32,5120]{1,0:T(8,128)(2,1)} copy(bf16[32,5120]{1,0:T(8,128)(2,1)} %attend_project.1) | data formatting | bytes 655360

commit v4 on v3

--- a/solution.py
+++ b/solution.py
@@ -24,7 +24,7 @@
 FEATURES = HEADS * HEAD
 EXP2_SCALE = HEAD**-0.5 * math.log2(math.e)
 MESH = pl.DeviceIdType.MESH
-CUTS = (0, 2, 4, 6)
+CUTS = (2, 4, 6, 8)
 ROW_BLOCKS = tuple(NZ * (row + 1) for row in range(NY))
 SENT = (24, 16, 22, 14)
 HOPS_Z = (0, 1, 1, 2, 2)
@@ -256,11 +256,11 @@
 
 
 def kernel(
-    vert_hbm, count_hbm, slash_hbm, q_hbm, k_hbm, v_hbm, w_hbm, out_hbm,
+    vert_hbm, count_hbm, slash_hbm, q_hbm, k_hbm, v_hbm, w_hbm, out_ref,
     keys_vm, values_vm, q_vm, w_vm, scores, weights, scale_by, att, part,
-    opp_in, dir_in, sum_in, sum_out, out_vm,
+    opp_in, dir_in, sum_in, sum_out,
     vert_ref, count_ref, slash_ref, key_at, value_at, bias_at,
-    full_sem, half_sem, send_sem, twin_send, twin_recv, own_sem, q_sem, w_sem, out_sem,
+    full_sem, half_sem, send_sem, twin_send, twin_recv, own_sem, q_sem, w_sem,
     opp_sem, dir_sem, sum_sem, first_send, second_send,
 ):
     me, tp = lax.axis_index("seq"), lax.axis_index("tp")
@@ -375,23 +375,23 @@
                 + dir_in[p].astype(jnp.float32)
                 + sum_in[p].astype(jnp.float32)
             )
-            at = slice(p * PIECE, (p + 1) * PIECE)
-            out_vm[:, at] = whole.astype(jnp.bfloat16)
-            pltpu.make_async_copy(out_vm.at[:, at], out_hbm.at[:, at], out_sem).start()
+            out_ref[:, p * PIECE : (p + 1) * PIECE] = whole.astype(jnp.bfloat16)
     pltpu.make_async_copy(part.at[pl.ds(0, SIDE)], part.at[pl.ds(0, SIDE)], first_send).wait()
     pltpu.make_async_copy(sum_out, sum_out, second_send).wait()
     moves.sent()
-    pltpu.make_async_copy(out_vm, out_hbm, out_sem).wait()
 
 
 def body(queries, key_vectors, value_vectors, vertical, vertical_count, slash_offsets, out_weight):
     anywhere = pl.BlockSpec(memory_space=pl.ANY)
     bf16, dma = jnp.bfloat16, pltpu.SemaphoreType.DMA
+    inputs = (
+        vertical, vertical_count, slash_offsets, queries, key_vectors, value_vectors, out_weight
+    )
     return pl.pallas_call(
         kernel,
         out_shape=jax.ShapeDtypeStruct((ROWS, D), bf16),
         in_specs=[anywhere] * 7,
-        out_specs=anywhere,
+        out_specs=pl.BlockSpec(memory_space=pltpu.VMEM),
         scratch_shapes=[
             pltpu.VMEM((NB, BLOCK, HEAD), bf16),
             pltpu.VMEM((NB, BLOCK, HEAD), bf16),
@@ -406,7 +406,6 @@
             pltpu.VMEM((PIECES, ROWS, PIECE), bf16),
             pltpu.VMEM((PIECES, ROWS, PIECE), bf16),
             pltpu.VMEM((PIECES, ROWS, PIECE), bf16),
-            pltpu.VMEM((ROWS, D), bf16),
             pltpu.SMEM((HEADS, NVERT), jnp.int32),
             pltpu.SMEM((HEADS,), jnp.int32),
             pltpu.SMEM((HEADS, NSLASH), jnp.int32),
@@ -421,7 +420,6 @@
             dma((5,)),
             dma,
             dma((PIECES,)),
-            dma,
             dma((PIECES,)),
             dma((PIECES,)),
             dma((PIECES,)),
@@ -429,13 +427,13 @@
             dma,
         ],
         compiler_params=pltpu.CompilerParams(
-            collective_id=0, has_side_effects=True, vmem_limit_bytes=64 * 1024 * 1024
+            collective_id=0, has_side_effects=True, vmem_limit_bytes=48 * 1024 * 1024
         ),
         cost_estimate=pl.CostEstimate(
             flops=3_200_000_000, bytes_accessed=16_000_000, transcendentals=3_300_000
         ),
         name="attend_project",
-    )(vertical, vertical_count, slash_offsets, queries, key_vectors, value_vectors, out_weight)
+    )(*[pltpu.with_memory_space_constraint(a, pltpu.HBM) for a in inputs])
 
 
 def solution(mesh):

time: 50.1 us -> 47.4 us (0.946); the launches traced: 49.5 us -> 47.3 us
  Pallas kernels: 47.8 us -> 46.6 us
  local copies, waits for them, and re-layouts: 1.72 us -> 0.73 us
    pallas_call x1, Pallas kernels: 47.8 us -> 46.6 us  [body(): pl.pallas_call(kernel, out_shape=jax.ShapeDtypeStruct((ROWS, D), bf16), i...]
    unnamed x1, local copies, waits for them, and re-layouts: 1.72 us -> 0.73 us
where the time goes in v4:
time: 47.4 us; the launch traced here: 47.3 us
  Pallas kernels  46.6 us (98%)
  local copies, waits for them, and re-layouts  0.73 us (2%)
    pallas_call x1, Pallas kernels, body(): pl.pallas_call(kernel, out_shape=jax.ShapeDtypeStruct((ROWS, D), bf16), i...  46.6 us

profile of v4, /device:TPU:24, one launch (start us, length us, event | category | flops | bytes accessed | tf_op | source)
XLA Modules:
  0.0 47.3 jit_solution(16370856041308383581)
XLA Ops:
  0.0 46.6 %attend_project.1 = bf16[32,5120]{1,0:T(8,128)(2,1)S(1)} custom-call(s32[8,16]{1,0:T(8,128)} %vert_hbm.1, s32[8]{0:T(128)} %count_hbm.1, s32[8,8]{1,0:T(8,128)} %slash_hbm.1, bf16[128,1024]{1,0:T(8,128)(2,1)} %q_hbm.1, bf16[128,128]{1,0:T(8,128)(2,1)} %k_hbm.1, bf16[128,128]{1,0:T(8,128)(2,1)} %v_hbm.1, bf16[1024,5120]{1,0:T(8,128)(2,1)} %w_hbm.1), custom_call_target="tpu_custom_call" | custom-call | flops 3200000000 | bytes 16000000 | tf_op jit(solution)/shard_map/attend_project/pallas_call | solution.py:390
  46.6 0.7 %copy.9 = bf16[32,5120]{1,0:T(8,128)(2,1)} copy(bf16[32,5120]{1,0:T(8,128)(2,1)S(1)} %attend_project.1) | data formatting | bytes 655360

commit v5 on v4

--- a/solution.py
+++ b/solution.py
@@ -98,16 +98,19 @@
     scale_by[head] = jnp.broadcast_to(1.0 / total, (BLOCK, HEAD))
 
 
-def combine_head(head, values_vm, value_at, own_value, weights, scale_by, att):
+def combine_head(head, half, starts, values_vm, value_at, own_value, weights, scale_by, att):
+    def of_targets(ref, at):
+        return jnp.concatenate([ref[head, pl.ds(start, ROWS), at] for start in starts], axis=0)
+
     out = None
     for slots in slot_groups(4):
         values = [values_vm[own_value if s == 0 else value_at[head, s]] for s in slots]
         values = values[0] if len(values) == 1 else jnp.concatenate(values, axis=0)
-        part = weights[head, :, slots[0] * BLOCK : (slots[-1] + 1) * BLOCK]
+        part = of_targets(weights, slice(slots[0] * BLOCK, (slots[-1] + 1) * BLOCK))
         term = jnp.dot(part, values, preferred_element_type=jnp.float32)
         out = term if out is None else out + term
-    out = out * scale_by[head]
-    att[:, pl.ds(pl.multiple_of(head * HEAD, HEAD), HEAD)] = out.astype(jnp.bfloat16)
+    out = out * of_targets(scale_by, slice(0, HEAD))
+    att[half, :, pl.ds(pl.multiple_of(head * HEAD, HEAD), HEAD)] = out.astype(jnp.bfloat16)
 
 
 def remote(src, dst, send, recv, where):
@@ -340,29 +343,52 @@
     do(ends[cuts[HEADS // 2] :])
     moves.other_half(1)
 
-    @pl.loop(0, HEADS // 2)
-    def _(pair):
-        for n in range(2):
-            combine_head(pair * 2 + n, values_vm, value_at, own_value, weights, scale_by, att)
-
-    def rows_of(p, target):
-        return part.at[p, pl.ds(pl.multiple_of((target + 4) % 4 * ROWS, ROWS), ROWS)]
+    starts = [
+        [pl.multiple_of((tp + ahead) % 4 * ROWS, ROWS) for ahead in pair]
+        for pair in ((2, 1), (3, 0))
+    ]
+    first, second = pl.ds(0, ROWS), pl.ds(ROWS, ROWS)
+
+    def project(half, p):
+        part[half, p] = jnp.dot(
+            att[half], w_vm[p], preferred_element_type=jnp.float32
+        ).astype(jnp.bfloat16)
+
+    def combine(half):
+        @pl.loop(0, HEADS // 2)
+        def _(pair):
+            for n in range(2):
+                combine_head(
+                    pair * 2 + n, half, starts[half], values_vm, value_at, own_value,
+                    weights, scale_by, att,
+                )
+
+    def send_direct(half, rows, p, where):
+        remote(part.at[half, p, rows], dir_in.at[p], first_send, dir_sem.at[p], where).start()
+
+    combine(0)
 
     @pl.loop(0, SIDE)
     def _(j):
-        for p, ahead, behind, step in ((j, right, left, 1), (j + SIDE, left, right, -1)):
+        for p, ahead in ((j, right), (j + SIDE, left)):
             pltpu.make_async_copy(w_vm.at[p], w_vm.at[p], w_sem.at[p]).wait()
-            part[p] = jnp.dot(att[...], w_vm[p], preferred_element_type=jnp.float32).astype(
-                jnp.bfloat16
-            )
-            remote(rows_of(p, tp + 2), opp_in.at[p], first_send, opp_sem.at[p], ahead).start()
-            remote(rows_of(p, tp - step), dir_in.at[p], first_send, dir_sem.at[p], behind).start()
+            project(0, p)
+            remote(part.at[0, p, first], opp_in.at[p], first_send, opp_sem.at[p], ahead).start()
+        send_direct(0, second, j + SIDE, right)
+
+    combine(1)
 
     @pl.loop(0, SIDE)
     def _(j):
-        for p, ahead, step in ((j, right, 1), (j + SIDE, left, -1)):
+        project(1, j)
+        send_direct(1, first, j, left)
+        project(1, j + SIDE)
+
+    @pl.loop(0, SIDE)
+    def _(j):
+        for p, ahead, half, rows in ((j, right, 0, second), (j + SIDE, left, 1, first)):
             pltpu.make_async_copy(opp_in.at[p], opp_in.at[p], opp_sem.at[p]).wait()
-            summed = opp_in[p].astype(jnp.float32) + rows_of(p, tp + step)[...].astype(jnp.float32)
+            summed = opp_in[p].astype(jnp.float32) + part[half, p, rows].astype(jnp.float32)
             sum_out[p] = summed.astype(jnp.bfloat16)
             remote(sum_out.at[p], sum_in.at[p], second_send, sum_sem.at[p], ahead).start()
 
@@ -371,12 +397,12 @@
             pltpu.make_async_copy(dir_in.at[p], dir_in.at[p], dir_sem.at[p]).wait()
             pltpu.make_async_copy(sum_in.at[p], sum_in.at[p], sum_sem.at[p]).wait()
             whole = (
-                rows_of(p, tp)[...].astype(jnp.float32)
+                part[1, p, second].astype(jnp.float32)
                 + dir_in[p].astype(jnp.float32)
                 + sum_in[p].astype(jnp.float32)
             )
             out_ref[:, p * PIECE : (p + 1) * PIECE] = whole.astype(jnp.bfloat16)
-    pltpu.make_async_copy(part.at[pl.ds(0, SIDE)], part.at[pl.ds(0, SIDE)], first_send).wait()
+    pltpu.make_async_copy(part.at[0], part.at[0], first_send).wait()
     pltpu.make_async_copy(sum_out, sum_out, second_send).wait()
     moves.sent()
 
@@ -400,8 +426,8 @@
             pltpu.VMEM((2, BLOCK, SLOTS * BLOCK), jnp.float32),
             pltpu.VMEM((HEADS, BLOCK, SLOTS * BLOCK), bf16),
             pltpu.VMEM((HEADS, BLOCK, HEAD), jnp.float32),
-            pltpu.VMEM((BLOCK, FEATURES), bf16),
-            pltpu.VMEM((PIECES, BLOCK, PIECE), bf16),
+            pltpu.VMEM((2, 2 * ROWS, FEATURES), bf16),
+            pltpu.VMEM((2, PIECES, 2 * ROWS, PIECE), bf16),
             pltpu.VMEM((PIECES, ROWS, PIECE), bf16),
             pltpu.VMEM((PIECES, ROWS, PIECE), bf16),
             pltpu.VMEM((PIECES, ROWS, PIECE), bf16),

time: 47.4 us -> 47.2 us (level)
  no operation moved by 1% of the time
where the time goes in v5:
time: 47.2 us; the launch traced here: 47.1 us
  Pallas kernels  46.4 us (98%)
  local copies, waits for them, and re-layouts  0.73 us (2%)
    pallas_call x1, Pallas kernels, body(): pl.pallas_call(kernel, out_shape=jax.ShapeDtypeStruct((ROWS, D), bf16), i...  46.4 us

profile of v5, /device:TPU:24, one launch (start us, length us, event | category | flops | bytes accessed | tf_op | source)
XLA Modules:
  0.0 47.1 jit_solution(14110649561844529469)
XLA Ops:
  0.0 46.4 %attend_project.1 = bf16[32,5120]{1,0:T(8,128)(2,1)S(1)} custom-call(s32[8,16]{1,0:T(8,128)} %vert_hbm.1, s32[8]{0:T(128)} %count_hbm.1, s32[8,8]{1,0:T(8,128)} %slash_hbm.1, bf16[128,1024]{1,0:T(8,128)(2,1)} %q_hbm.1, bf16[128,128]{1,0:T(8,128)(2,1)} %k_hbm.1, bf16[128,128]{1,0:T(8,128)(2,1)} %v_hbm.1, bf16[1024,5120]{1,0:T(8,128)(2,1)} %w_hbm.1), custom_call_target="tpu_custom_call" | custom-call | flops 3200000000 | bytes 16000000 | tf_op jit(solution)/shard_map/attend_project/pallas_call | solution.py:416
  46.4 0.7 %copy.9 = bf16[32,5120]{1,0:T(8,128)(2,1)} copy(bf16[32,5120]{1,0:T(8,128)(2,1)S(1)} %attend_project.1) | data formatting | bytes 655360

commit v6 on v5

--- a/solution.py
+++ b/solution.py
@@ -286,17 +286,6 @@
             )
         )
     ]
-    for copy in own_copies:
-        copy.start()
-    for head in range(HEADS):
-        pltpu.make_async_copy(
-            q_hbm.at[:, pl.ds(head * HEAD, HEAD)], q_vm.at[head], q_sem
-        ).start()
-    for p in range(PIECES):
-        pltpu.make_async_copy(
-            w_hbm.at[:, pl.ds(p * PIECE, PIECE)], w_vm.at[p], w_sem.at[p]
-        ).start()
-
     moves = Gather(
         (keys_vm, values_vm), (full_sem, half_sem, send_sem, twin_send, twin_recv),
         (k_hbm, v_hbm), core, y, z, seq_at,
@@ -307,6 +296,8 @@
     )
     for where in neighbours:
         pl.semaphore_signal(barrier, inc=1, device_id=where, device_id_type=MESH)
+    for copy in own_copies:
+        copy.start()
     pl.semaphore_wait(barrier, len(neighbours))
 
     keys, values = moves.stages(0), moves.stages(1)
@@ -317,6 +308,14 @@
 
     do(keys[0])
     do(values[0])
+    for head in range(HEADS):
+        pltpu.make_async_copy(
+            q_hbm.at[:, pl.ds(head * HEAD, HEAD)], q_vm.at[head], q_sem
+        ).start()
+    for p in range(PIECES):
+        pltpu.make_async_copy(
+            w_hbm.at[:, pl.ds(p * PIECE, PIECE)], w_vm.at[p], w_sem.at[p]
+        ).start()
     for copy in own_copies:
         copy.wait()
 

time: 47.2 us -> 46.5 us (0.985)
  Pallas kernels: 46.4 us -> 45.6 us
    pallas_call x1, Pallas kernels: 46.4 us -> 45.6 us  [body(): pl.pallas_call(kernel, out_shape=jax.ShapeDtypeStruct((ROWS, D), bf16), i...]
where the time goes in v6:
time: 46.5 us; the launch traced here: 46.3 us
  Pallas kernels  45.6 us (98%)
  local copies, waits for them, and re-layouts  0.73 us (2%)
    pallas_call x1, Pallas kernels, body(): pl.pallas_call(kernel, out_shape=jax.ShapeDtypeStruct((ROWS, D), bf16), i...  45.6 us

profile of v6, /device:TPU:24, one launch (start us, length us, event | category | flops | bytes accessed | tf_op | source)
XLA Modules:
  0.0 46.3 jit_solution(1625076845857481343)
XLA Ops:
  0.0 45.6 %attend_project.1 = bf16[32,5120]{1,0:T(8,128)(2,1)S(1)} custom-call(s32[8,16]{1,0:T(8,128)} %vert_hbm.1, s32[8]{0:T(128)} %count_hbm.1, s32[8,8]{1,0:T(8,128)} %slash_hbm.1, bf16[128,1024]{1,0:T(8,128)(2,1)} %q_hbm.1, bf16[128,128]{1,0:T(8,128)(2,1)} %k_hbm.1, bf16[128,128]{1,0:T(8,128)(2,1)} %v_hbm.1, bf16[1024,5120]{1,0:T(8,128)(2,1)} %w_hbm.1), custom_call_target="tpu_custom_call" | custom-call | flops 3200000000 | bytes 16000000 | tf_op jit(solution)/shard_map/attend_project/pallas_call | solution.py:415
  45.6 0.7 %copy.9 = bf16[32,5120]{1,0:T(8,128)(2,1)} copy(bf16[32,5120]{1,0:T(8,128)(2,1)S(1)} %attend_project.1) | data formatting | bytes 655360
